TPU v7x, 256 devices: a whole 4x4x8 slice. The times are simulated.
256 devices in a mesh: ctx: 64 (over x, z, core), head: 4 (over y).
Axes of the slice: x: 4, y: 4, z: 8, core: 2. Of those that a mesh axis runs over, the one named last changes fastest.
Arguments:
- query: bfloat16 [4096, 64, 192], P('ctx', 'head'), may hold values from -110 to 110
- w_uk: bfloat16 [64, 128, 512], P('head'), may hold values from -0.5 to 0.5
- w_uv: bfloat16 [64, 512, 128], P('head'), may hold values from -0.25 to 0.25
- index_query: bfloat16 [4096, 64, 128], P('ctx', 'head'), may hold values from -1.25 to 1.25
- index_weight: float32 [4096, 64], P('ctx', 'head'), may hold values from -2 to 2
- cache_rows: bfloat16 [131072, 704], P('ctx'), may hold values from -16 to 16
- key_scale: float32 [131072], P('ctx'), may hold values from 0.25 to 4
- selected: int32 [4096, 32], P('ctx'), may hold values from 0 to 2047, as said below
- block_home: int32 [2048], replicated, may hold values from 0 to 2047, as said below
Outputs:
- attn_out: bfloat16 [4096, 64, 128], P('ctx', 'head')
- index_scores: float32 [4096, 2048], P('ctx', 'head')
Inputs may be any that keep to these rules, and one draw needn't show every extreme that they name: `selected`: each query names 32 distinct blocks. The queries of one ctx device together name exactly 64 distinct blocks, at most 2 of which sit in the shard of any one ctx device; in every draw one ctx device's shard holds 2 of the blocks of every device. `block_home`: A permutation of the physical blocks.
All inputs are finite; a program needn't handle non-finite values.
Results may differ from a plain program's by a relative error of at most 0.015.
Values may be sent and summed in bfloat16 or wider, within the bound.
A program may use at most 128 MiB of HBM per device.

v0:
```python
import jax
import jax.numpy as jnp
from jax import lax
from jax.sharding import PartitionSpec as P

LATENT = 512
ROPE = 64
HEAD_DIM = 128
BLOCK = 64
NSEL = 32
POOL = 64
BLK_DEV = 32


def shards(
    query, w_uk, w_uv, index_query, index_weight, cache_rows, key_scale, selected, block_home
):
    ctx_count = lax.axis_size("ctx")
    width = cache_rows.shape[1]
    capacity = 2 * POOL // ctx_count
    block_total = block_home.shape[0]
    score_scale = query.shape[-1] ** (-0.5)
    q_nope = query[..., :HEAD_DIM]
    q_rope = query[..., HEAD_DIM:]
    q_lat = jnp.einsum("thd,hdc->thc", q_nope, w_uk, preferred_element_type=jnp.float32).astype(
        jnp.bfloat16
    )
    q_joined = jnp.concatenate([q_lat, q_rope], axis=-1)
    wanted = jnp.zeros((block_total,), jnp.int32).at[selected.reshape(-1)].set(1)
    wanted_phys = jnp.zeros((block_total,), jnp.int32).at[block_home].set(wanted)
    owner_grid = wanted_phys.reshape(ctx_count, BLK_DEV)
    rank_flat = (jnp.cumsum(owner_grid, axis=1) - 1).reshape(-1)
    pool_pos = jnp.cumsum(wanted_phys) - 1
    all_blocks = jnp.arange(block_total, dtype=jnp.int32)
    owner_of = all_blocks // BLK_DEV
    slot_of = all_blocks % BLK_DEV
    is_wanted = wanted_phys == 1
    requests = (
        jnp.zeros((ctx_count, capacity), jnp.int32)
        .at[owner_of, jnp.where(is_wanted, rank_flat, capacity)]
        .set(slot_of, mode="drop")
    )
    buffer_pos = owner_of * capacity + rank_flat
    pool_source = (
        jnp.zeros((POOL,), jnp.int32)
        .at[jnp.where(is_wanted, pool_pos, POOL)]
        .set(buffer_pos, mode="drop")
    )
    sel_pool = pool_pos[block_home[selected]]
    incoming = lax.all_to_all(requests, "ctx", split_axis=0, concat_axis=0, tiled=True)
    local_blocks = cache_rows.reshape(BLK_DEV, BLOCK * width)
    local_scale = key_scale.reshape(BLK_DEV, BLOCK)
    served = jnp.take(local_blocks, incoming, axis=0)
    served_scale = jnp.take(local_scale, incoming, axis=0)
    fetched, fetched_scale = (
        lax.all_to_all(served, "ctx", split_axis=0, concat_axis=0, tiled=True),
        lax.all_to_all(
            served_scale.astype(jnp.bfloat16), "ctx", split_axis=0, concat_axis=0, tiled=True
        ).astype(served_scale.dtype),
    )
    fetched = fetched.reshape(ctx_count * capacity, BLOCK * width)
    fetched_scale = fetched_scale.reshape(ctx_count * capacity, BLOCK)
    pool_keys = jnp.take(fetched, pool_source, axis=0).reshape(POOL * BLOCK, width)
    pool_scale = jnp.take(fetched_scale, pool_source, axis=0).reshape(POOL * BLOCK)
    latent = pool_keys[:, :LATENT]
    score_keys = pool_keys[:, : LATENT + ROPE]
    index_keys = pool_keys[:, LATENT + ROPE :]
    member = jnp.any(
        sel_pool[:, :, None] == jnp.arange(POOL, dtype=jnp.int32)[None, None, :], axis=1
    )
    mask_bias = jnp.where(jnp.repeat(member, BLOCK, axis=1), 0.0, -jnp.inf).astype(jnp.float32)[
        :, None, :
    ]
    scores = (
        jnp.einsum("thc,sc->ths", q_joined, score_keys, preferred_element_type=jnp.float32)
        * score_scale
        + mask_bias
    )
    top = jnp.max(scores, axis=-1, keepdims=True)
    expo = jnp.exp(scores - top)
    probs = (expo / jnp.sum(expo, axis=-1, keepdims=True)).astype(jnp.bfloat16)
    context = jnp.einsum("ths,sc->thc", probs, latent, preferred_element_type=jnp.float32).astype(
        jnp.bfloat16
    )
    attn_out = jnp.einsum("thc,hcd->thd", context, w_uv, preferred_element_type=jnp.float32).astype(
        jnp.bfloat16
    )
    raw = jnp.einsum("tjd,sd->tjs", index_query, index_keys, preferred_element_type=jnp.float32)
    weighted = (
        jnp.sum(index_weight[:, :, None] * jnp.maximum(raw, 0.0), axis=1) * pool_scale[None, :]
    )
    weighted = weighted.reshape(weighted.shape[0], POOL, BLOCK)
    picked = jnp.take_along_axis(weighted, sel_pool[:, :, None], axis=1)
    picked = picked.reshape(picked.shape[0], NSEL * BLOCK)
    index_scores = lax.psum_scatter(
        picked.astype(jnp.bfloat16), "head", scatter_dimension=1, tiled=True
    ).astype(jnp.float32)
    return (attn_out, index_scores)


def solution(mesh):
    return jax.shard_map(
        shards,
        mesh=mesh,
        in_specs=(
            P("ctx", "head", None),
            P("head", None, None),
            P("head", None, None),
            P("ctx", "head", None),
            P("ctx", "head"),
            P("ctx", None),
            P("ctx"),
            P("ctx", None),
            P(),
        ),
        out_specs=(P("ctx", "head", None), P("ctx", "head")),
        check_vma=False,
    )
```

profile of v0, /device:TPU:1, one launch (start us, length us, event | category | flops | bytes accessed | tf_op | source)
XLA Modules:
  0.0 520.7 jit_solution(12305672704987888431)
XLA Ops:
  7.2 0.9 copy.54
  8.2 0.7 compare_select_fusion.8
  9.0 8.0 %scatter_custom_fusion = s32[2048]{0:T(1024)S(1)} fusion(s32[2048]{0:T(1024)S(1)} %bitcast.48, s32[2048]{0:T(1024)S(1)} %broadcast.268, s32[]{:T(128)} %constant.110.clone.1), kind=kCustom, calls=%fused_computation.87 | custom fusion | bytes 8196 | tf_op jit(solution)/shard_map/scatter | solution.py:29
  17.0 8.0 %scatter_custom_fusion.1 = s32[2048]{0:T(1024)S(1)} fusion(s32[2048]{0:T(1024)S(1)} %compare_select_fusion.8, s32[2048]{0:T(1024)S(1)} %scatter_custom_fusion, s32[]{:T(128)} %constant.110.clone.1), kind=kCustom, calls=%fused_computation.85 | custom fusion | bytes 8196 | tf_op jit(solution)/shard_map/scatter | solution.py:30
  25.1 0.3 reduce-window.9
  26.0 0.7 multiply_reduce_fusion.1
  26.8 0.8 and_reduce_fusion
  27.6 8.0 %scatter_custom_fusion.3 = s32[128]{0:T(128)S(1)} fusion(s32[2048]{0:T(1024)S(1)} %get-tuple-element.18, s32[2048]{0:T(1024)S(1)} %get-tuple-element.17, s32[]{:T(128)} %constant.110.clone.1), kind=kCustom, calls=%fused_computation.94 | custom fusion | bytes 516
  35.7 0.7 copy.55
  36.4 13.0 %all-to-all-start = ((s32[64,1,2]{2,1,0:T(1,128)}), s32[64,1,2]{2,1,0:T(1,128)S(1)}, u32[]{:S(2)}, u32[]{:S(2)}) async-start(s32[64,1,2]{2,1,0:T(1,128)} %copy.55), calls=%async_computation | async-start | bytes 65536 | tf_op jit(solution)/shard_map/all_to_all | solution.py:50
  49.4 4.6 copy.58
  54.0 6.4 %reshape.233 = bf16[32,45056]{1,0:T(8,128)(2,1)} reshape(bf16[2048,704]{1,0:T(8,128)(2,1)} %copy.58) | data formatting | bytes 5767168 | tf_op jit(solution)/shard_map/reshape | solution.py:51
  60.9 24.6 %gather_fusion = bf16[128,45056]{1,0:T(8,128)(2,1)} fusion(bf16[32,45056]{1,0:T(8,128)(2,1)} %reshape.233, s32[1024]{0:T(1024)S(1)} %pad_clamp_fusion.1), kind=kCustom, calls=%fused_computation | custom fusion | bytes 23069184 | tf_op jit(solution)/shard_map/jit(_take)/gather | solution.py:53
  85.4 16.2 %reshape.245 = bf16[64,2,45056]{2,1,0:T(2,128)(2,1)} reshape(bf16[128,45056]{1,0:T(8,128)(2,1)} %gather_fusion) | data formatting | bytes 23068672 | tf_op jit(solution)/shard_map/jit(_take)/gather | solution.py:53
  101.8 0.7 gather_fusion.4
  102.5 0.8 select_convert_fusion.1
  103.2 10.3 %all-to-all-start.2 = ((bf16[64,2,64]{2,1,0:T(2,128)(2,1)}), bf16[64,2,64]{2,1,0:T(2,128)(2,1)S(1)}, u32[]{:S(2)}, u32[]{:S(2)}) async-start(bf16[64,2,64]{2,1,0:T(2,128)(2,1)} %select_convert_fusion.1), calls=%async_computation.2 | async-start | bytes 65536 | tf_op jit(solution)/shard_map/all_to_all | solution.py:57
  113.5 14.9 %broadcast_select_fusion = bf16[64,2,45056]{2,1,0:T(2,128)(2,1)} fusion(bf16[64,2,45056]{2,1,0:T(2,128)(2,1)} %reshape.245, pred[64,2]{1,0:T(8,128)(4,1)S(1)} %copy.57), kind=kLoop, calls=%fused_computation.12 | loop fusion | flops 5767168 | bytes 23068800 | tf_op jit(solution)/shard_map/jit(_take)/select_n | solution.py:53
  128.5 10.6 %all-to-all-start.1 = ((bf16[64,2,45056]{2,1,0:T(2,128)(2,1)}), bf16[64,2,45056]{2,1,0:T(2,128)(2,1)}, u32[]{:S(2)}, u32[]{:S(2)}) async-start(bf16[64,2,45056]{2,1,0:T(2,128)(2,1)} %broadcast_select_fusion), calls=%async_computation.1 | async-start | bytes 23068672 | tf_op jit(solution)/shard_map/all_to_all | solution.py:56
  139.2 0.7 slice.22
  140.0 11.8 %gather_fusion.2 = s32[2048]{0:T(1024)S(1)} fusion(s32[2048]{0:T(1024)S(1)} %copy-done.2, s32[2048]{0:T(1024)S(1)} %broadcast_clamp_fusion), kind=kCustom, calls=%fused_computation.2 | custom fusion | bytes 24576 | tf_op jit(solution)/shard_map/gather | solution.py:49
  152.0 11.8 %gather_fusion.3 = s32[2048]{0:T(1024)S(1)} fusion(s32[2048]{0:T(1024)S(1)} %get-tuple-element.11, s32[2048]{0:T(1024)S(1)} %broadcast_clamp_fusion.1), kind=kCustom, calls=%fused_computation.3 | custom fusion | bytes 24576 | tf_op jit(solution)/shard_map/gather | solution.py:49
  163.9 8.2 %scatter_custom_fusion.2 = s32[64]{0:T(128)S(1)} fusion(s32[2048]{0:T(1024)S(1)} %get-tuple-element.10, s32[2048]{0:T(1024)S(1)} %get-tuple-element.13, s32[]{:T(128)} %constant.110.clone.1), kind=kCustom, calls=%fused_computation.96 | custom fusion | bytes 260 | tf_op jit(solution)/shard_map/scatter | solution.py:47
  172.1 0.5 copy-done.9
  172.9 0.4 fusion.11
  173.3 2.0 broadcast_in_dim.118
  175.3 2.1 select_n.168
  177.5 0.7 compare_select_fusion.11
  178.2 1.4 fusion.7
  179.8 0.6 gather_fusion.5
  180.4 211.9 %all-to-all-done.1 = bf16[64,2,45056]{2,1,0:T(2,128)(2,1)} async-done(((bf16[64,2,45056]{2,1,0:T(2,128)(2,1)}), bf16[64,2,45056]{2,1,0:T(2,128)(2,1)}, u32[]{:S(2)}, u32[]{:S(2)}) %all-to-all-start.1) | async-done | bytes 11534368 | tf_op jit(solution)/shard_map/all_to_all | solution.py:56
  392.3 15.2 %reshape.234 = bf16[128,45056]{1,0:T(8,128)(2,1)} reshape(bf16[64,2,45056]{2,1,0:T(2,128)(2,1)} %all-to-all-done.1) | data formatting | bytes 23068672 | tf_op jit(solution)/shard_map/reshape | solution.py:61
  407.5 17.4 %gather_fusion.1 = bf16[64,45056]{1,0:T(8,128)(2,1)} fusion(bf16[128,45056]{1,0:T(8,128)(2,1)} %reshape.234, s32[1024]{0:T(1024)S(1)} %pad_clamp_fusion), kind=kCustom, calls=%fused_computation.1 | custom fusion | bytes 11534592 | tf_op jit(solution)/shard_map/jit(_take)/gather | solution.py:63
  424.9 11.2 %gather.34 = bf16[4096,704]{1,0:T(8,128)(2,1)} reshape(bf16[64,45056]{1,0:T(8,128)(2,1)} %gather_fusion.1) | data formatting | bytes 11534336 | tf_op jit(solution)/shard_map/jit(_take)/gather | solution.py:63
  436.1 8.6 %copy.61 = bf16[4096,704]{0,1:T(8,128)(2,1)} copy(bf16[4096,704]{1,0:T(8,128)(2,1)} %gather.34) | data formatting | bytes 11534336 | tf_op jit(solution)/shard_map/jit(_take)/gather | solution.py:63
  444.7 3.2 broadcast_select_fusion.1
  448.0 10.3 %fusion.5 = f32[64,16,4096]{2,1,0:T(8,128)} fusion(bf16[4096,704]{0,1:T(8,128)(2,1)S(1)} %broadcast_select_fusion.1, bf16[64,16,576]{2,0,1:T(8,128)(2,1)S(1)} %pad_maximum_fusion), kind=kOutput, calls=%fused_computation.23 | convolution fusion | flops 4831838208 | bytes 22806528 | tf_op jit(solution)/shard_map/thc,sc->ths/dot_general | solution.py:75
  458.3 2.6 multiply_reduce_fusion
  460.9 2.2 reduce_sum.25
  463.1 1.9 broadcast_multiply_fusion
  465.0 11.1 %gather_fusion.6 = bf16[2048,64]{1,0:T(8,128)(2,1)S(1)} fusion(bf16[64,64,64]{2,1,0:T(8,128)(2,1)S(1)} %broadcast_multiply_fusion, s32[2048]{0:T(1024)S(1)} %reshape.292), kind=kCustom, calls=%fused_computation.6 | custom fusion | bytes 540672 | tf_op jit(solution)/shard_map/jit(take_along_axis)/gather | solution.py:93
  476.1 0.3 select_convert_fusion
  476.4 1.2 convert_element_type.39
  477.6 20.5 %fusion.35 = (f32[64,16]{1,0:T(8,128)S(1)}, f32[64,16,4096]{2,1,0:T(8,128)}) fusion(f32[64,16,4096]{2,1,0:T(8,128)} %fusion.5, f32[64,4096]{1,0:T(8,128)S(1)} %select_n.168), kind=kOutput, calls=%fused_computation.99 | output fusion | flops 25169920 | bytes 34607104 | tf_op jit(solution)/shard_map/sub | solution.py:80
  498.2 11.7 %fusion.6 = bf16[64,16,512]{2,1,0:T(8,128)(2,1)S(1)} fusion(bf16[4096,704]{0,1:T(8,128)(2,1)} %copy-done.3, f32[64,16,4096]{2,1,0:T(8,128)} %get-tuple-element.16, f32[64,16]{1,0:T(8,128)S(1)} %get-tuple-element.15), kind=kOutput, calls=%fused_computation.25 | convolution fusion | flops 4303880192 | bytes 22024192 | tf_op jit(solution)/shard_map/ths,sc->thc/dot_general | solution.py:82
  509.8 1.3 fusion.9
  511.2 0.9 copy.71
  512.1 1.5 convert_element_type.40
  (70 shorter events, 2.5 us)
Async XLA Ops:
  7.2 171.0 %copy-start = (bf16[16,128,512]{2,1,0:T(8,128)(2,1)S(1)}, bf16[16,128,512]{2,1,0:T(8,128)(2,1)}, u32[]{:S(2)}) copy-start(bf16[16,128,512]{2,1,0:T(8,128)(2,1)} %param.10) | copy-start | bytes 6291460
  36.4 24.1 %all-to-all-start = ((s32[64,1,2]{2,1,0:T(1,128)}), s32[64,1,2]{2,1,0:T(1,128)S(1)}, u32[]{:S(2)}, u32[]{:S(2)}) async-start(s32[64,1,2]{2,1,0:T(1,128)} %copy.55), calls=%async_computation | async-start | bytes 65536 | tf_op jit(solution)/shard_map/all_to_all | solution.py:50
  49.4 11.0 %copy-start.6 = (f32[2048]{0:T(1024)S(1)}, f32[2048]{0:T(1024)}, u32[]{:S(2)}) copy-start(f32[2048]{0:T(1024)} %param.15) | copy-start | bytes 24580
  103.2 25.2 %all-to-all-start.2 = ((bf16[64,2,64]{2,1,0:T(2,128)(2,1)}), bf16[64,2,64]{2,1,0:T(2,128)(2,1)S(1)}, u32[]{:S(2)}, u32[]{:S(2)}) async-start(bf16[64,2,64]{2,1,0:T(2,128)(2,1)} %select_convert_fusion.1), calls=%async_computation.2 | async-start | bytes 65536 | tf_op jit(solution)/shard_map/all_to_all | solution.py:57
  128.5 10.7 %copy-start.5 = (bf16[64,16,192]{2,1,0:T(8,128)(2,1)S(1)}, bf16[64,16,192]{2,1,0:T(8,128)(2,1)}, u32[]{:S(2)}) copy-start(bf16[64,16,192]{2,1,0:T(8,128)(2,1)} %param.9) | copy-start | bytes 1179652
  128.5 263.8 %all-to-all-start.1 = ((bf16[64,2,45056]{2,1,0:T(2,128)(2,1)}), bf16[64,2,45056]{2,1,0:T(2,128)(2,1)}, u32[]{:S(2)}, u32[]{:S(2)}) async-start(bf16[64,2,45056]{2,1,0:T(2,128)(2,1)} %broadcast_select_fusion), calls=%async_computation.1 | async-start | bytes 23068672 | tf_op jit(solution)/shard_map/all_to_all | solution.py:56
  139.1 0.9 copy-start.2
  139.1 372.9 %reduce-scatter.2.cloned.1.call-start = ((), (), s32[]{:S(2)}) async-start(), calls=%async_computation.4 | async-start | bytes 327680 | tf_op jit(solution)/shard_map/reduce_scatter | solution.py:95
  152.0 20.8 %slice-start = ((bf16[64,16,192]{2,1,0:T(8,128)(2,1)}), bf16[64,16,64]{2,1,0:T(8,128)(2,1)S(1)}, s32[]{:S(2)}) async-start(bf16[64,16,192]{2,1,0:T(8,128)(2,1)} %param.9), calls=%async_computation.5 | async-start | bytes 524288 | tf_op jit(solution)/shard_map/slice | solution.py:24
  172.1 0.5 copy-start.9
  447.9 10.4 %copy-start.3 = (bf16[4096,704]{0,1:T(8,128)(2,1)}, bf16[4096,704]{0,1:T(8,128)(2,1)S(1)}, u32[]{:S(2)}) copy-start(bf16[4096,704]{0,1:T(8,128)(2,1)S(1)} %broadcast_select_fusion.1) | copy-start | bytes 17301508
  447.9 10.4 %copy-start.7 = (bf16[64,16,128]{2,1,0:T(8,128)(2,1)S(1)}, bf16[64,16,128]{2,1,0:T(8,128)(2,1)}, u32[]{:S(2)}) copy-start(bf16[64,16,128]{2,1,0:T(8,128)(2,1)} %param.12) | copy-start | bytes 786436
  447.9 10.3 %copy-start.8 = (f32[64,16]{0,1:T(8,128)S(1)}, f32[64,16]{0,1:T(8,128)}, u32[]{:S(2)}) copy-start(f32[64,16]{0,1:T(8,128)} %param.13) | copy-start | bytes 12292
  498.2 11.7 %copy-start.4 = (bf16[16,512,128]{2,1,0:T(8,128)(2,1)S(1)}, bf16[16,512,128]{2,1,0:T(8,128)(2,1)}, u32[]{:S(2)}) copy-start(bf16[16,512,128]{2,1,0:T(8,128)(2,1)} %param.11) | copy-start | bytes 6291460
  498.2 15.4 %copy-start.1 = (bf16[16,128,512]{2,1,0:T(8,128)(2,1)S(1)}, bf16[16,128,512]{2,1,0:T(8,128)(2,1)}, u32[]{:S(2)}) copy-start(bf16[16,128,512]{2,1,0:T(8,128)(2,1)} %param.10) | copy-start | bytes 6291460
Sparse Core Ops, SparseCore 0:
  477.7 17.7 reduce-scatter.1
where the time goes:
time: 527 us; the launch traced here: 521 us
  waiting for transfers between devices  212 us (40%)
  local copies, waits for them, and re-layouts  185 us (35%)
  other arithmetic  47.3 us (9%)
  starting transfers between devices  34 us (6%)
  matrix products  27.3 us (5%)
  between operations  14.7 us (3%)
    all_to_all x1, waiting for transfers between devices, shards(): lax.all_to_all(served, 'ctx', split_axis=0, concat_axis=0, tiled=True)  212 us
    gather x2, local copies, waits for them, and re-layouts, shards(): served = jnp.take(local_blocks, incoming, axis=0)  40.8 us
    gather x3, local copies, waits for them, and re-layouts, shards(): jnp.take(fetched, pool_source, axis=0).reshape(POOL * BLOCK, width)  37.2 us
    gather x5, local copies, waits for them, and re-layouts, shards(): sel_pool = pool_pos[block_home[selected]]  23.8 us
    sub x1, other arithmetic, shards(): expo = jnp.exp(scores - top)  20.5 us
    reshape x1, local copies, waits for them, and re-layouts, shards(): fetched = fetched.reshape(ctx_count * capacity, BLOCK * width)  15.2 us
    unnamed x26, local copies, waits for them, and re-layouts  15.2 us
    select_n x2, other arithmetic, shards(): served = jnp.take(local_blocks, incoming, axis=0)  14.9 us
  transfers between devices with their start and end apart: 4, of which 1 were waited for; matrix products, arithmetic and copies ran while one was open for 19% of the time, Pallas kernels for 0%

commit v1 on v0

v1 whole, which is shorter than its diff:
```python
import jax
import jax.numpy as jnp
from jax import lax
from jax.experimental import pallas as pl
from jax.experimental.pallas import tpu as pltpu
from jax.sharding import PartitionSpec as P

LATENT = 512
ROPE = 64
HEAD_DIM = 128
IDX_DIM = 128
BLOCK = 64
NSEL = 32
POOL = 64
BLK_DEV = 32
NBLK = 2048
Q_DEV = 64
HEADS_DEV = 16
CTX_DEVS = 64
HEAD_DEVS = 4
PART = BLOCK // HEAD_DEVS
ROWS = HEADS_DEV * Q_DEV
PART_KEYS = POOL * PART
HALF = PART_KEYS // 2
PAIR = 2 * LATENT + 2 * IDX_DIM + 2 * ROPE
NEG = -1e30
MESH = pl.DeviceIdType.MESH
BF = jnp.bfloat16
F32 = jnp.float32


def nn(a, b):
    return jnp.dot(a, b, preferred_element_type=F32)


def nt(a, b):
    return lax.dot_general(a, b, (((1,), (1,)), ((), ())), preferred_element_type=F32)


def iota(shape, dim):
    return lax.broadcasted_iota(jnp.int32, shape, dim)


def onehot(cond):
    return jnp.where(cond, 1.0, 0.0).astype(BF)


def kernel(
    sel_ref,
    home_ref,
    scale_ref,
    iw_ref,
    query_hbm,
    iq_hbm,
    cache_hbm,
    wuk_hbm,
    wuv_hbm,
    attn_ref,
    idx_ref,
    cache_v,
    query_v,
    iq_v,
    wuk_v,
    wuv_v,
    want,
    want_in,
    weights,
    expand,
    served,
    recv,
    posn,
    bias,
    pack0,
    pack1,
    ukeys,
    kv,
    rp,
    iq_all,
    iw_all,
    qlat,
    qra,
    qrb,
    wsum,
    picked,
    picked_in,
    top,
    total,
    acc,
    local_sem,
    req_send,
    req_recv,
    blk_send,
    blk_recv,
    iq_send,
    iq_recv,
    iw_send,
    iw_recv,
    pk_send,
    pk_recv,
    ag_send,
    ag_recv,
    fw_send,
    fw_recv,
):
    me = lax.axis_index("ctx")
    y = lax.axis_index("head")

    def ctx_peer(c):
        return (lax.rem(c + 2 * CTX_DEVS, CTX_DEVS), y)

    def head_peer(d):
        return (me, lax.rem(y + d, HEAD_DEVS))

    barrier = pltpu.get_barrier_semaphore()

    @pl.loop(1, CTX_DEVS)
    def _(s):
        pl.semaphore_signal(barrier, inc=1, device_id=ctx_peer(me + s), device_id_type=MESH)

    for d in range(1, HEAD_DEVS):
        pl.semaphore_signal(barrier, inc=1, device_id=head_peer(d), device_id_type=MESH)

    rows16 = pl.ds(pl.multiple_of(y * PART, PART), PART)
    cp_cache = pltpu.make_async_copy(cache_hbm.at[:, rows16, :], cache_v, local_sem.at[0])
    cp_query = pltpu.make_async_copy(query_hbm, query_v, local_sem.at[1])
    cp_iq = pltpu.make_async_copy(iq_hbm, iq_v, local_sem.at[2])
    cp_wuk = pltpu.make_async_copy(wuk_hbm, wuk_v, local_sem.at[3])
    cp_wuv = pltpu.make_async_copy(wuv_hbm, wuv_v, local_sem.at[4])
    for cp in (cp_cache, cp_query, cp_iq, cp_wuk, cp_wuv):
        cp.start()

    sel = sel_ref[...]
    home = home_ref[...]
    sel_hi = onehot(iota((32, NBLK), 0) == (sel >> 6))
    sel_lo = onehot(iota((64, NBLK), 0) == (sel & 63))
    lane = iota((1, NBLK), 1)
    log_hi = onehot(iota((32, NBLK), 0) == (lane >> 6))
    log_lo = onehot(iota((64, NBLK), 0) == (lane & 63))
    counts = nt(sel_hi, sel_lo)
    wanted = onehot(counts > 0.5)
    wanted_row = jnp.sum(nn(wanted, log_lo) * log_hi.astype(F32), axis=0, keepdims=True)
    rel = (me - (home >> 5)) & (CTX_DEVS - 1)
    holder = jnp.where(iota((CTX_DEVS, NBLK), 0) == rel, 1.0, 0.0)
    slot = onehot(iota((128, NBLK), 0) == (home & (BLK_DEV - 1)))
    want_rel = nt((holder * wanted_row).astype(BF), slot)
    want[...] = want_rel.reshape(CTX_DEVS, 1, 128)
    want_in[0] = want[0]

    pl.semaphore_wait(barrier, CTX_DEVS - 1 + HEAD_DEVS - 1)

    def request(s):
        return pltpu.make_async_remote_copy(
            src_ref=want.at[s],
            dst_ref=want_in.at[s],
            send_sem=req_send.at[s],
            recv_sem=req_recv.at[s],
            device_id=ctx_peer(me - s),
            device_id_type=MESH,
        )

    @pl.loop(1, CTX_DEVS)
    def _(s):
        request(s).start()

    cp_cache.wait()
    rows = cache_v[...].reshape(BLK_DEV * PART, LATENT + ROPE + IDX_DIM)
    pick_scale = iota((BLK_DEV, PART, BLOCK), 2) == y * PART + iota((BLK_DEV, PART, BLOCK), 1)
    scale3 = jnp.broadcast_to(scale_ref[...][:, None, :], (BLK_DEV, PART, BLOCK))
    scale_col = jnp.sum(jnp.where(pick_scale, scale3, 0.0), axis=2, keepdims=True)
    scale_col = scale_col.reshape(BLK_DEV * PART, 1)
    tail = rows[:, LATENT:].astype(F32)
    tail_lane = iota(tail.shape, 1)
    tail = (tail * jnp.where(tail_lane >= ROPE, scale_col, 1.0)).astype(BF)
    src = iota((ROPE + IDX_DIM, 384), 0)
    dst = iota((ROPE + IDX_DIM, 384), 1)
    arrange = onehot(
        ((dst < 128) & (src == dst + ROPE))
        | ((dst >= 128) & (dst < 192) & (src == dst - 128))
        | ((dst >= 320) & (src == dst - 320))
    )
    weights[:, :LATENT] = rows[:, :LATENT]
    weights[:, LATENT:] = nn(tail, arrange).astype(BF)

    @pl.loop(1, CTX_DEVS)
    def _(s):
        request(s).wait_recv()

    asked = want_in[...].reshape(CTX_DEVS, 128)
    before = onehot(iota((128, 128), 0) < iota((128, 128), 1))
    order = nn(asked.astype(BF), before)
    spread = onehot(iota((128, 512), 0) == (iota((128, 512), 1) >> 4))
    for k in range(2):
        first = jnp.where(jnp.abs(order - float(k)) < 0.5, asked, 0.0)
        expand[k] = nn(first.astype(BF), spread)

    def block_copy(s):
        return pltpu.make_async_remote_copy(
            src_ref=served.at[s],
            dst_ref=recv.at[s],
            send_sem=blk_send.at[s],
            recv_sem=blk_recv.at[s],
            device_id=ctx_peer(me + s),
            device_id_type=MESH,
        )

    group = 16

    @pl.loop(0, CTX_DEVS // group)
    def _(i):
        at = pl.ds(pl.multiple_of(i * group, group), group)
        same_row = iota((1, PART, 512), 1) == (iota((1, PART, 512), 2) & (PART - 1))
        gather = []
        for k in range(2):
            wide = jnp.where(same_row, expand[k, at, :][:, None, :], 0.0)
            gather.append(wide.reshape(group * PART, 512).astype(BF))
        o0 = nn(gather[0], weights[:, : LATENT + 256]).astype(BF)
        o1 = nn(gather[1], weights[:, : LATENT + IDX_DIM]).astype(BF)
        r1 = nn(gather[1], weights[:, LATENT + 256 :]).astype(BF)
        shape = (group, PART, -1)
        served[at, :, 0:512] = o0[:, :512].reshape(shape)
        served[at, :, 512:1024] = o1[:, :512].reshape(shape)
        served[at, :, 1024:1152] = o0[:, 512:640].reshape(shape)
        served[at, :, 1152:1280] = o1[:, 512:640].reshape(shape)
        served[at, :, 1280:1408] = (o0[:, 640:768] + r1).reshape(shape)

        @pl.loop(jnp.where(i == 0, 1, 0), group)
        def _(j):
            block_copy(i * group + j).start()

    recv[0] = served[0]

    cp_query.wait()
    cp_iq.wait()
    cp_wuk.wait()
    col = iota((HEAD_DIM + ROPE, 384), 0)
    out = iota((HEAD_DIM + ROPE, 384), 1)
    q_arrange = onehot(
        ((out < 192) & (col == out)) | ((out >= 320) & (col == out - 320 + HEAD_DIM))
    )

    @pl.loop(0, HEADS_DEV)
    def _(h):
        rows_h = pl.ds(pl.multiple_of(h * Q_DEV, Q_DEV), Q_DEV)
        take = onehot(
            iota((Q_DEV, ROWS), 1) == iota((Q_DEV, ROWS), 0) * HEADS_DEV + h
        )
        iq_all[y, rows_h, :] = nn(take, iq_v[...].reshape(ROWS, IDX_DIM)).astype(BF)

    iw_all[y] = iw_ref[...]

    def iq_copy(d):
        return pltpu.make_async_remote_copy(
            src_ref=iq_all.at[y],
            dst_ref=iq_all.at[y],
            send_sem=iq_send.at[d - 1],
            recv_sem=iq_recv.at[d - 1],
            device_id=head_peer(d),
            device_id_type=MESH,
        )

    def iw_copy(d):
        return pltpu.make_async_remote_copy(
            src_ref=iw_all.at[y],
            dst_ref=iw_all.at[y],
            send_sem=iw_send.at[d - 1],
            recv_sem=iw_recv.at[d - 1],
            device_id=head_peer(d),
            device_id_type=MESH,
        )

    for d in range(1, HEAD_DEVS):
        iq_copy(d).start()
        iw_copy(d).start()

    @pl.loop(0, HEADS_DEV)
    def _(h):
        rows_h = pl.ds(pl.multiple_of(h * Q_DEV, Q_DEV), Q_DEV)
        take = onehot(
            iota((Q_DEV, ROWS), 1) == iota((Q_DEV, ROWS), 0) * HEADS_DEV + h
        )
        mine = nn(take, query_v[...].reshape(ROWS, HEAD_DIM + ROPE)).astype(BF)
        parts = nn(mine, q_arrange).astype(BF)
        qlat[rows_h, :] = nn(parts[:, :HEAD_DIM], wuk_v[h]).astype(BF)
        qra[rows_h, :] = parts[:, 128:256]
        qrb[rows_h, :] = parts[:, 256:384]

    asked_rel = want[...].reshape(CTX_DEVS, 128).astype(BF)
    rank = nn(asked_rel, before)
    row_count = nn(asked_rel, jnp.ones((128, 128), BF))
    earlier = onehot(iota((CTX_DEVS, CTX_DEVS), 1) < iota((CTX_DEVS, CTX_DEVS), 0))
    ahead = nn(earlier, row_count.astype(BF))
    place = asked_rel.astype(F32) * (ahead + rank + 1.0)
    place_row = jnp.sum(nn(place.astype(BF), slot) * holder, axis=0, keepdims=True)
    place_log = nt(log_lo, (log_hi.astype(F32) * place_row).astype(BF))
    looked = nn(place_log.astype(BF), sel_hi) * sel_lo.astype(F32)
    pos_sel = jnp.sum(looked, axis=0, keepdims=True)
    member = jnp.zeros((POOL, 128), F32)
    pool_id = iota((POOL, 128), 0).astype(F32) + 1.0
    for i in range(NSEL // 2):
        part = pos_sel[:, i * 128 : (i + 1) * 128]
        posn[i : i + 1, :] = part
        member = member + jnp.where(jnp.abs(pool_id - part) < 0.5, 1.0, 0.0)
    member = member + pltpu.roll(member, 64, 1)
    member = jnp.concatenate([member, jnp.zeros((128 - POOL, 128), F32)], axis=0).T[:Q_DEV, :]
    to_keys = onehot(iota((128, PART_KEYS), 0) == (iota((128, PART_KEYS), 1) >> 4))
    bias[...] = jnp.where(nn(member.astype(BF), to_keys) > 0.5, 0.0, NEG)

    count_lane = nt(jnp.ones((8, 128), BF), asked_rel)
    ahead_lane = nn(
        count_lane.astype(BF), onehot(iota((CTX_DEVS, CTX_DEVS), 0) < iota((CTX_DEVS, CTX_DEVS), 1))
    )
    count_lane = count_lane[0:1, :]
    ahead_lane = ahead_lane[0:1, :]
    lane_of = onehot(iota((CTX_DEVS, PART_KEYS), 0) == (iota((CTX_DEVS, PART_KEYS), 1) >> 4))
    pool_row = iota((POOL, CTX_DEVS), 0).astype(F32)
    for k, pack in ((0, pack0), (1, pack1)):
        hit = (jnp.abs(ahead_lane + float(k) - pool_row) < 0.5) & (count_lane > k + 0.5)
        pack[...] = nn(onehot(hit), lane_of)

    top[...] = jnp.full(top.shape, NEG, F32)
    total[...] = jnp.zeros(total.shape, F32)
    acc[...] = jnp.zeros(acc.shape, F32)

    @pl.loop(1, CTX_DEVS)
    def _(s):
        block_copy(s).wait_recv()

    def direct(way, half, what):
        ref = (kv, rp)[what]
        return pltpu.make_async_remote_copy(
            src_ref=ref.at[y, half],
            dst_ref=ref.at[y, half],
            send_sem=ag_send.at[way, half, what],
            recv_sem=ag_recv.at[way, half, what],
            device_id=head_peer((1, 3)[way]),
            device_id_type=MESH,
        )

    def forward(way, what):
        ref = (kv, rp)[what]
        origin = lax.rem(y + (3, 1)[way], HEAD_DEVS)
        return pltpu.make_async_remote_copy(
            src_ref=ref.at[origin, way],
            dst_ref=ref.at[origin, way],
            send_sem=fw_send.at[way, what],
            recv_sem=fw_recv.at[way, what],
            device_id=head_peer((1, 3)[way]),
            device_id_type=MESH,
        )

    dup = onehot((iota((128, 128), 0) & 63) == (iota((128, 128), 1) & 63))
    low = iota((1, 128), 1) < ROPE
    for half in range(2):
        same_row = iota((1, PART, PART_KEYS), 1) == (iota((1, PART, PART_KEYS), 2) & (PART - 1))
        compact = []
        for pack in (pack0, pack1):
            wide = jnp.where(same_row, pack[half * 32 : half * 32 + 32, :][:, None, :], 0.0)
            compact.append(wide.reshape(HALF, PART_KEYS).astype(BF))
        flat = recv[...].reshape(PART_KEYS, PAIR)
        kv[y, half] = (
            nn(compact[0], flat[:, 0:512]) + nn(compact[1], flat[:, 512:1024])
        ).astype(BF)
        ropes = flat[:, 1280:1408]
        ropes0 = jnp.where(low, ropes, jnp.zeros_like(ropes))
        ropes1 = jnp.where(low, jnp.zeros_like(ropes), ropes)
        twice = nn(
            (nn(compact[0], ropes0) + nn(compact[1], ropes1)).astype(BF), dup
        ).astype(BF)
        rp[y, half] = jnp.where(low, twice[: HALF // 2], twice[HALF // 2 :])
        for way in range(2):
            for what in range(2):
                direct(way, half, what).start()
        ukeys[half * HALF : half * HALF + HALF, :] = (
            nn(compact[0], flat[:, 1024:1152]) + nn(compact[1], flat[:, 1152:1280])
        ).astype(BF)

    for d in range(1, HEAD_DEVS):
        iq_copy(d).wait_recv()
        iw_copy(d).wait_recv()

    @pl.loop(0, 4)
    def _(i):
        keys_at = pl.ds(pl.multiple_of(i * 256, 256), 256)
        keys = ukeys[keys_at, :]

        def heads(j, sums):
            part = lax.div(j, 4)
            quad = lax.rem(j, 4)
            queries = iq_all[part, pl.ds(pl.multiple_of(quad * 256, 256), 256), :]
            raw = jnp.maximum(nt(keys, queries), 0.0)
            return (
                sums
                + raw[:, :128] * iw_all[part, pl.ds(quad * 2, 1), :]
                + raw[:, 128:] * iw_all[part, pl.ds(quad * 2 + 1, 1), :]
            )

        sums = lax.fori_loop(0, 16, heads, jnp.zeros((256, 128), F32))
        wsum[pl.ds(pl.multiple_of(i * 16, 16), 16)] = (sums + pltpu.roll(sums, 64, 1)).reshape(
            16, PART, 128
        )

    @pl.loop(0, NSEL // 2)
    def _(i):
        at = posn[pl.ds(i, 1), :] - 1.0
        ids = iota((POOL, PART, 128), 0).astype(F32)
        chosen = jnp.where(jnp.abs(ids - at[None]) < 0.5, wsum[...], 0.0)
        picked[i] = jnp.sum(chosen, axis=0)

    def picked_copy(d):
        to = lax.rem(y + d, HEAD_DEVS)
        return pltpu.make_async_remote_copy(
            src_ref=picked.at[pl.ds(to * 4, 4)],
            dst_ref=picked_in.at[y],
            send_sem=pk_send.at[d - 1],
            recv_sem=pk_recv.at[d - 1],
            device_id=head_peer(d),
            device_id_type=MESH,
        )

    for d in range(1, HEAD_DEVS):
        picked_copy(d).start()
    picked_in[y] = picked[pl.ds(y * 4, 4)]

    factor = (HEAD_DIM + ROPE) ** -0.5 * 1.4426950408889634

    @pl.loop(0, 8)
    def _(step):
        for k, way, half in ((2, 0, 0), (3, 1, 0), (4, 0, 1), (5, 1, 1)):

            @pl.when(step == k)
            def _():
                for what in range(2):
                    direct(way, half, what).wait_recv()
                    if way == half:
                        forward(way, what).start()

        for k, way in ((6, 0), (7, 1)):

            @pl.when(step == k)
            def _():
                for what in range(2):
                    forward(way, what).wait_recv()

        side = jnp.where(lax.rem(step, 2) == 0, 3, 1)
        ahead_y = jnp.where(step < 2, 0, jnp.where(step < 6, side, 2))
        origin = lax.rem(y + ahead_y, HEAD_DEVS)
        half = jnp.where(
            step < 2, step, jnp.where(step < 6, lax.div(step - 2, 2), step - 6)
        )

        @pl.loop(0, 4)
        def _(g):
            at = pl.ds(pl.multiple_of(g * 256, 256), 256)
            keys = kv[origin, half]
            ropes = rp[origin, half]
            scores = nt(qlat[at, :], keys)
            scores = scores + jnp.concatenate([nt(qra[at, :], ropes), nt(qrb[at, :], ropes)], axis=1)
            masked = bias[:, pl.ds(pl.multiple_of(half * HALF, HALF), HALF)]
            scores = (scores.reshape(4, Q_DEV, HALF) + masked[None]).reshape(256, HALF)
            old = top[at, :]
            new = jnp.maximum(old, jnp.max(scores, axis=1, keepdims=True))
            expo = jnp.exp2((scores - new) * factor)
            keep = jnp.exp2((old - new) * factor)
            total[at, :] = total[at, :] * keep + jnp.sum(expo, axis=1, keepdims=True)
            acc[at, :] = acc[at, :] * keep + nn(expo.astype(BF), keys)
            top[at, :] = new

    cp_wuv.wait()
    for h in range(HEADS_DEV):
        at = slice(h * Q_DEV, h * Q_DEV + Q_DEV)
        context = (acc[at, :] / total[at, :]).astype(BF)
        attn_ref[:, h * HEAD_DIM : (h + 1) * HEAD_DIM] = nn(context, wuv_v[h]).astype(BF)

    for d in range(1, HEAD_DEVS):
        picked_copy(d).wait_recv()
    for i in range(4):
        even = jnp.concatenate([picked_in[j, i] for j in range(HEAD_DEVS)], axis=0)
        both = jnp.concatenate([even, pltpu.roll(even, 64, 1)], axis=0)
        idx_ref[:, i * 128 : (i + 1) * 128] = both.T[:Q_DEV, :]

    @pl.loop(1, CTX_DEVS)
    def _(s):
        request(s).wait_send()
        block_copy(s).wait_send()

    for d in range(1, HEAD_DEVS):
        iq_copy(d).wait_send()
        iw_copy(d).wait_send()
        picked_copy(d).wait_send()
    for way in range(2):
        for what in range(2):
            for half in range(2):
                direct(way, half, what).wait_send()
            forward(way, what).wait_send()


def shards(
    query, w_uk, w_uv, index_query, index_weight, cache_rows, key_scale, selected, block_home
):
    vmem = pl.BlockSpec(memory_space=pltpu.VMEM)
    hbm = pl.BlockSpec(memory_space=pl.ANY)
    dma = pltpu.SemaphoreType.DMA
    width = cache_rows.shape[1]
    attn, idx = pl.pallas_call(
        kernel,
        out_shape=(
            jax.ShapeDtypeStruct((Q_DEV, HEADS_DEV * HEAD_DIM), BF),
            jax.ShapeDtypeStruct((Q_DEV, NSEL * BLOCK // HEAD_DEVS), F32),
        ),
        in_specs=[vmem] * 4 + [hbm] * 5,
        out_specs=(vmem, vmem),
        scratch_shapes=[
            pltpu.VMEM((BLK_DEV, PART, width), BF),
            pltpu.VMEM(query.shape, BF),
            pltpu.VMEM(index_query.shape, BF),
            pltpu.VMEM(w_uk.shape, BF),
            pltpu.VMEM(w_uv.shape, BF),
            pltpu.VMEM((CTX_DEVS, 1, 128), F32),
            pltpu.VMEM((CTX_DEVS, 1, 128), F32),
            pltpu.VMEM((BLK_DEV * PART, LATENT + 384), BF),
            pltpu.VMEM((2, CTX_DEVS, 512), F32),
            pltpu.VMEM((CTX_DEVS, PART, PAIR), BF),
            pltpu.VMEM((CTX_DEVS, PART, PAIR), BF),
            pltpu.VMEM((NSEL // 2, 128), F32),
            pltpu.VMEM((Q_DEV, PART_KEYS), F32),
            pltpu.VMEM((POOL, PART_KEYS), F32),
            pltpu.VMEM((POOL, PART_KEYS), F32),
            pltpu.VMEM((PART_KEYS, IDX_DIM), BF),
            pltpu.VMEM((HEAD_DEVS, 2, HALF, LATENT), BF),
            pltpu.VMEM((HEAD_DEVS, 2, HALF // 2, 128), BF),
            pltpu.VMEM((HEAD_DEVS, ROWS, IDX_DIM), BF),
            pltpu.VMEM((HEAD_DEVS, 8, 128), F32),
            pltpu.VMEM((ROWS, LATENT), BF),
            pltpu.VMEM((ROWS, 128), BF),
            pltpu.VMEM((ROWS, 128), BF),
            pltpu.VMEM((POOL, PART, 128), F32),
            pltpu.VMEM((NSEL // 2, PART, 128), F32),
            pltpu.VMEM((HEAD_DEVS, NSEL // 8, PART, 128), F32),
            pltpu.VMEM((ROWS, 1), F32),
            pltpu.VMEM((ROWS, 1), F32),
            pltpu.VMEM((ROWS, LATENT), F32),
            dma((5,)),
            dma((CTX_DEVS,)),
            dma((CTX_DEVS,)),
            dma((CTX_DEVS,)),
            dma((CTX_DEVS,)),
            dma((3,)),
            dma((3,)),
            dma((3,)),
            dma((3,)),
            dma((3,)),
            dma((3,)),
            dma((2, 2, 2)),
            dma((2, 2, 2)),
            dma((2, 2)),
            dma((2, 2)),
        ],
        compiler_params=pltpu.CompilerParams(
            collective_id=0, has_side_effects=True, vmem_limit_bytes=58 * 1024 * 1024
        ),
    )(
        selected.T.reshape(1, Q_DEV * NSEL),
        block_home.reshape(1, NBLK),
        key_scale.reshape(BLK_DEV, BLOCK),
        index_weight.T.reshape(8, 128),
        query,
        index_query,
        cache_rows.reshape(BLK_DEV, BLOCK, width),
        w_uk,
        w_uv,
    )
    return (attn.reshape(Q_DEV, HEADS_DEV, HEAD_DIM), idx)


def solution(mesh):
    return jax.shard_map(
        shards,
        mesh=mesh,
        in_specs=(
            P("ctx", "head", None),
            P("head", None, None),
            P("head", None, None),
            P("ctx", "head", None),
            P("ctx", "head"),
            P("ctx", None),
            P("ctx"),
            P("ctx", None),
            P(),
        ),
        out_specs=(P("ctx", "head", None), P("ctx", "head")),
        check_vma=False,
    )
```

time: 527 us -> 157 us (0.30); the launches traced: 521 us -> 157 us
  waiting for transfers between devices: 212 us -> 0 us
  local copies, waits for them, and re-layouts: 185 us -> 12 us
  Pallas kernels: 0 us -> 144 us
  other arithmetic: 47.3 us -> 0 us
  starting transfers between devices: 34 us -> 0 us
  matrix products: 27.3 us -> 0 us
  between operations: 14.7 us -> 0.64 us
    all_to_all x3 -> x0, waiting for transfers between devices: 212 us -> none  [the longest x1 212 us: shards(): lax.all_to_all(served, 'ctx', split_axis=0, concat_axis=0, tiled=True)]
    pallas_call x0 -> x1, Pallas kernels: none -> 144 us  [shards(): pl.pallas_call(kernel, out_shape=(jax.ShapeDtypeStruct((Q_DEV, HEADS_DEV...]
    gather x14 -> x0, local copies, waits for them, and re-layouts: 114 us -> none  [the longest x2 40.8 us: shards(): served = jnp.take(local_blocks, incoming, axis=0)]
    all_to_all x3 -> x0, starting transfers between devices: 33.9 us -> none  [the longest x1 13 us: shards(): lax.all_to_all(requests, 'ctx', split_axis=0, concat_axis=0, tiled=True)]
    dot_general x5 -> x0, matrix products: 27.3 us -> none  [the longest x1 11.7 us: shards(): jnp.einsum('ths,sc->thc', probs, latent, preferred_element_type=jnp.float32)]
    scatter x3 -> x0, local copies, waits for them, and re-layouts: 24.3 us -> none  [the longest x1 8.21 us: shards(): pool_source = jnp.zeros((POOL,), jnp.int32).at[jnp.where(is_wanted, pool_...]
    sub x2 -> x0, other arithmetic: 20.5 us -> none  [the longest x1 20.5 us: shards(): expo = jnp.exp(scores - top)]
    select_n x13 -> x0, other arithmetic: 19.7 us -> none  [the longest x2 14.9 us: shards(): served = jnp.take(local_blocks, incoming, axis=0)]
  transfers between devices with their start and end apart: 4 -> 0, of which waited for: 1 -> 0; matrix products, arithmetic and copies ran while one was open for 19% -> 0% of each run, Pallas kernels for 0% -> 0%
where the time goes in v1:
time: 157 us
  Pallas kernels  144 us (92%)
  local copies, waits for them, and re-layouts  12 us (8%)
    pallas_call x1, Pallas kernels, shards(): pl.pallas_call(kernel, out_shape=(jax.ShapeDtypeStruct((Q_DEV, HEADS_DEV...  144 us
    unnamed x3, local copies, waits for them, and re-layouts  7.86 us

profile of v1, /device:TPU:1, one launch (start us, length us, event | category | flops | bytes accessed | tf_op | source)
XLA Modules:
  0.0 157.0 jit_solution(15982998068926108155)
XLA Ops:
  0.6 1.4 reshape.25.iw_ref
  2.0 1.4 reshape.22.sel_ref
  3.4 1.4 reshape.24.scale_ref
  4.8 4.6 %copy.11 = bf16[2048,704]{1,0:T(8,128)(2,1)} copy(bf16[2048,704]{0,1:T(8,128)(2,1)} %param.14) | data formatting | bytes 5767168 | tf_op args[5]
  9.3 144.3 %shard_map.104 = (bf16[64,2048]{1,0:T(8,128)(2,1)}, f32[64,512]{1,0:T(8,128)}) custom-call(s32[1,2048]{1,0:T(1,128)} %reshape.22.sel_ref, s32[1,2048]{1,0:T(1,128)} %bitcast.10, f32[32,64]{1,0:T(8,128)} %reshape.24.scale_ref, f32[8,128]{1,0:T(8,128)} %reshape.25.iw_ref, bf16[64,16,192]{2,1,0:T(8,128)(2,1)} %query_hbm.1, bf16[64,16,128]{2,1,0:T(8,128)(2,1)} %iq_hbm.1, ...), custom_call_target="tpu_custom_call" | custom-call | tf_op jit(solution)/shard_map/pallas_call | solution.py:504
  153.7 1.7 %copy.12 = bf16[8,8,16,128]{3,2,1,0:T(8,128)(2,1)} copy(bf16[8,8,16,128]{3,1,2,0:T(8,128)(2,1)} %bitcast.8) | data formatting | bytes 524288
  155.4 1.6 copy.14

commit v2 on v1

--- a/solution.py
+++ b/solution.py
@@ -21,7 +21,8 @@
 PART = BLOCK // HEAD_DEVS
 ROWS = HEADS_DEV * Q_DEV
 PART_KEYS = POOL * PART
-HALF = PART_KEYS // 2
+PARTS = 4
+PIECE = PART_KEYS // PARTS
 PAIR = 2 * LATENT + 2 * IDX_DIM + 2 * ROPE
 NEG = -1e30
 MESH = pl.DeviceIdType.MESH
@@ -62,6 +63,7 @@
     iq_v,
     wuk_v,
     wuv_v,
+    wuv_t,
     want,
     want_in,
     weights,
@@ -72,7 +74,6 @@
     bias,
     pack0,
     pack1,
-    ukeys,
     kv,
     rp,
     iq_all,
@@ -120,8 +121,7 @@
     for d in range(1, HEAD_DEVS):
         pl.semaphore_signal(barrier, inc=1, device_id=head_peer(d), device_id_type=MESH)
 
-    rows16 = pl.ds(pl.multiple_of(y * PART, PART), PART)
-    cp_cache = pltpu.make_async_copy(cache_hbm.at[:, rows16, :], cache_v, local_sem.at[0])
+    cp_cache = pltpu.make_async_copy(cache_hbm, cache_v, local_sem.at[0])
     cp_query = pltpu.make_async_copy(query_hbm, query_v, local_sem.at[1])
     cp_iq = pltpu.make_async_copy(iq_hbm, iq_v, local_sem.at[2])
     cp_wuk = pltpu.make_async_copy(wuk_hbm, wuk_v, local_sem.at[3])
@@ -129,7 +129,7 @@
     for cp in (cp_cache, cp_query, cp_iq, cp_wuk, cp_wuv):
         cp.start()
 
-    sel = sel_ref[...]
+    sel = jnp.concatenate([sel_ref[i : i + 1, :] for i in range(NSEL)], axis=1)
     home = home_ref[...]
     sel_hi = onehot(iota((32, NBLK), 0) == (sel >> 6))
     sel_lo = onehot(iota((64, NBLK), 0) == (sel & 63))
@@ -163,23 +163,16 @@
         request(s).start()
 
     cp_cache.wait()
-    rows = cache_v[...].reshape(BLK_DEV * PART, LATENT + ROPE + IDX_DIM)
-    pick_scale = iota((BLK_DEV, PART, BLOCK), 2) == y * PART + iota((BLK_DEV, PART, BLOCK), 1)
-    scale3 = jnp.broadcast_to(scale_ref[...][:, None, :], (BLK_DEV, PART, BLOCK))
-    scale_col = jnp.sum(jnp.where(pick_scale, scale3, 0.0), axis=2, keepdims=True)
-    scale_col = scale_col.reshape(BLK_DEV * PART, 1)
-    tail = rows[:, LATENT:].astype(F32)
-    tail_lane = iota(tail.shape, 1)
-    tail = (tail * jnp.where(tail_lane >= ROPE, scale_col, 1.0)).astype(BF)
-    src = iota((ROPE + IDX_DIM, 384), 0)
-    dst = iota((ROPE + IDX_DIM, 384), 1)
-    arrange = onehot(
-        ((dst < 128) & (src == dst + ROPE))
-        | ((dst >= 128) & (dst < 192) & (src == dst - 128))
-        | ((dst >= 320) & (src == dst - 320))
-    )
-    weights[:, :LATENT] = rows[:, :LATENT]
-    weights[:, LATENT:] = nn(tail, arrange).astype(BF)
+    row = iota((BLK_DEV * PART, NBLK), 0)
+    mine = onehot(iota((BLK_DEV * PART, NBLK), 1) == (row >> 4) * BLOCK + y * PART + (row & 15))
+    scaled = (cache_v[LATENT + ROPE :, :].astype(F32) * scale_ref[...]).astype(BF)
+    rope = cache_v[LATENT : LATENT + ROPE, :]
+    weights[:, :LATENT] = nt(mine, cache_v[:LATENT, :]).astype(BF)
+    weights[:, LATENT : LATENT + IDX_DIM] = nt(mine, scaled).astype(BF)
+    ropes = nt(mine, jnp.concatenate([rope, rope], axis=0)).astype(BF)
+    low = iota((1, 128), 1) < ROPE
+    weights[:, LATENT + 128 : LATENT + 256] = jnp.where(low, ropes, jnp.zeros_like(ropes))
+    weights[:, LATENT + 256 :] = jnp.where(low, jnp.zeros_like(ropes), ropes)
 
     @pl.loop(1, CTX_DEVS)
     def _(s):
@@ -232,21 +225,26 @@
     cp_query.wait()
     cp_iq.wait()
     cp_wuk.wait()
+    cp_wuv.wait()
     col = iota((HEAD_DIM + ROPE, 384), 0)
     out = iota((HEAD_DIM + ROPE, 384), 1)
     q_arrange = onehot(
         ((out < 192) & (col == out)) | ((out >= 320) & (col == out - 320 + HEAD_DIM))
     )
 
-    @pl.loop(0, HEADS_DEV)
-    def _(h):
-        rows_h = pl.ds(pl.multiple_of(h * Q_DEV, Q_DEV), Q_DEV)
-        take = onehot(
-            iota((Q_DEV, ROWS), 1) == iota((Q_DEV, ROWS), 0) * HEADS_DEV + h
-        )
-        iq_all[y, rows_h, :] = nn(take, iq_v[...].reshape(ROWS, IDX_DIM)).astype(BF)
-
-    iw_all[y] = iw_ref[...]
+    def by_head(g):
+        rows_g = iota((256, ROWS), 0)
+        want_row = (rows_g & (Q_DEV - 1)) * HEADS_DEV + g * 4 + (rows_g >> 6)
+        return onehot(iota((256, ROWS), 1) == want_row)
+
+    @pl.loop(0, 4)
+    def _(g):
+        at = pl.ds(pl.multiple_of(g * 256, 256), 256)
+        iq_all[y, :, at] = nn(by_head(g), iq_v[...].reshape(ROWS, IDX_DIM)).astype(BF).T
+
+    for i in range(HEADS_DEV // 2):
+        pair = [iw_ref[2 * i + k : 2 * i + k + 1, :] for k in range(2)]
+        iw_all[y, i : i + 1, :] = jnp.concatenate(pair, axis=1)
 
     def iq_copy(d):
         return pltpu.make_async_remote_copy(
@@ -272,17 +270,19 @@
         iq_copy(d).start()
         iw_copy(d).start()
 
+    @pl.loop(0, 4)
+    def _(g):
+        at = pl.ds(pl.multiple_of(g * 256, 256), 256)
+        mine = nn(by_head(g), query_v[...].reshape(ROWS, HEAD_DIM + ROPE)).astype(BF)
+        parts = nn(mine, q_arrange).astype(BF)
+        lat = [nn(parts[k * 64 : k * 64 + 64, :HEAD_DIM], wuk_v[g * 4 + k]) for k in range(4)]
+        qlat[:, at] = jnp.concatenate(lat, axis=0).astype(BF).T
+        qra[:, at] = parts[:, 128:256].T
+        qrb[:, at] = parts[:, 256:384].T
+
     @pl.loop(0, HEADS_DEV)
     def _(h):
-        rows_h = pl.ds(pl.multiple_of(h * Q_DEV, Q_DEV), Q_DEV)
-        take = onehot(
-            iota((Q_DEV, ROWS), 1) == iota((Q_DEV, ROWS), 0) * HEADS_DEV + h
-        )
-        mine = nn(take, query_v[...].reshape(ROWS, HEAD_DIM + ROPE)).astype(BF)
-        parts = nn(mine, q_arrange).astype(BF)
-        qlat[rows_h, :] = nn(parts[:, :HEAD_DIM], wuk_v[h]).astype(BF)
-        qra[rows_h, :] = parts[:, 128:256]
-        qrb[rows_h, :] = parts[:, 256:384]
+        wuv_t[h] = wuv_v[h].T
 
     asked_rel = want[...].reshape(CTX_DEVS, 128).astype(BF)
     rank = nn(asked_rel, before)
@@ -301,9 +301,8 @@
         posn[i : i + 1, :] = part
         member = member + jnp.where(jnp.abs(pool_id - part) < 0.5, 1.0, 0.0)
     member = member + pltpu.roll(member, 64, 1)
-    member = jnp.concatenate([member, jnp.zeros((128 - POOL, 128), F32)], axis=0).T[:Q_DEV, :]
-    to_keys = onehot(iota((128, PART_KEYS), 0) == (iota((128, PART_KEYS), 1) >> 4))
-    bias[...] = jnp.where(nn(member.astype(BF), to_keys) > 0.5, 0.0, NEG)
+    allowed = jnp.broadcast_to(member[:, None, :], (POOL, PART, 128)).reshape(PART_KEYS, 128)
+    bias[...] = jnp.where(allowed > 0.5, 0.0, NEG)
 
     count_lane = nt(jnp.ones((8, 128), BF), asked_rel)
     ahead_lane = nn(
@@ -321,83 +320,129 @@
     total[...] = jnp.zeros(total.shape, F32)
     acc[...] = jnp.zeros(acc.shape, F32)
 
-    @pl.loop(1, CTX_DEVS)
-    def _(s):
-        block_copy(s).wait_recv()
-
-    def direct(way, half, what):
-        ref = (kv, rp)[what]
+    def direct(way, part, what):
+        ref, size = ((kv, PIECE), (rp, PIECE // 2))[what]
+        at = ref.at[y, pl.ds(part * size, size)]
         return pltpu.make_async_remote_copy(
-            src_ref=ref.at[y, half],
-            dst_ref=ref.at[y, half],
-            send_sem=ag_send.at[way, half, what],
-            recv_sem=ag_recv.at[way, half, what],
+            src_ref=at,
+            dst_ref=at,
+            send_sem=ag_send.at[way, part, what],
+            recv_sem=ag_recv.at[way, part, what],
             device_id=head_peer((1, 3)[way]),
             device_id_type=MESH,
         )
 
-    def forward(way, what):
-        ref = (kv, rp)[what]
+    def forward(way, part, what):
+        ref, size = ((kv, PIECE), (rp, PIECE // 2))[what]
         origin = lax.rem(y + (3, 1)[way], HEAD_DEVS)
+        at = ref.at[origin, pl.ds(part * size + way * (size // 2), size // 2)]
         return pltpu.make_async_remote_copy(
-            src_ref=ref.at[origin, way],
-            dst_ref=ref.at[origin, way],
-            send_sem=fw_send.at[way, what],
-            recv_sem=fw_recv.at[way, what],
+            src_ref=at,
+            dst_ref=at,
+            send_sem=fw_send.at[way, part, what],
+            recv_sem=fw_recv.at[way, part, what],
             device_id=head_peer((1, 3)[way]),
             device_id_type=MESH,
         )
 
     dup = onehot((iota((128, 128), 0) & 63) == (iota((128, 128), 1) & 63))
-    low = iota((1, 128), 1) < ROPE
-    for half in range(2):
-        same_row = iota((1, PART, PART_KEYS), 1) == (iota((1, PART, PART_KEYS), 2) & (PART - 1))
-        compact = []
+
+    def compact(part):
+        blocks = 32 + 8 * (part + 1)
+        depth = blocks * PART
+        at = slice(part * 16, part * 16 + 16)
+        same_row = iota((1, PART, depth), 1) == (iota((1, PART, depth), 2) & (PART - 1))
+        move = []
         for pack in (pack0, pack1):
-            wide = jnp.where(same_row, pack[half * 32 : half * 32 + 32, :][:, None, :], 0.0)
-            compact.append(wide.reshape(HALF, PART_KEYS).astype(BF))
-        flat = recv[...].reshape(PART_KEYS, PAIR)
-        kv[y, half] = (
-            nn(compact[0], flat[:, 0:512]) + nn(compact[1], flat[:, 512:1024])
+            wide = jnp.where(same_row, pack[at, :depth][:, None, :], 0.0)
+            move.append(wide.reshape(PIECE, depth).astype(BF))
+        flat = recv[:blocks].reshape(depth, PAIR)
+        kv[y, part * PIECE : part * PIECE + PIECE, :] = (
+            nn(move[0], flat[:, 0:512]) + nn(move[1], flat[:, 512:1024])
         ).astype(BF)
         ropes = flat[:, 1280:1408]
         ropes0 = jnp.where(low, ropes, jnp.zeros_like(ropes))
         ropes1 = jnp.where(low, jnp.zeros_like(ropes), ropes)
-        twice = nn(
-            (nn(compact[0], ropes0) + nn(compact[1], ropes1)).astype(BF), dup
-        ).astype(BF)
-        rp[y, half] = jnp.where(low, twice[: HALF // 2], twice[HALF // 2 :])
+        twice = nn((nn(move[0], ropes0) + nn(move[1], ropes1)).astype(BF), dup).astype(BF)
+        rp[y, part * (PIECE // 2) : (part + 1) * (PIECE // 2), :] = jnp.where(
+            low, twice[: PIECE // 2], twice[PIECE // 2 :]
+        )
         for way in range(2):
             for what in range(2):
-                direct(way, half, what).start()
-        ukeys[half * HALF : half * HALF + HALF, :] = (
-            nn(compact[0], flat[:, 1024:1152]) + nn(compact[1], flat[:, 1152:1280])
-        ).astype(BF)
-
+                direct(way, part, what).start()
+        return (nn(move[0], flat[:, 1024:1152]) + nn(move[1], flat[:, 1152:1280])).astype(BF)
+
+    def pass_on(part):
+        for way in range(2):
+            for what in range(2):
+                direct(way, part, what).wait_recv()
+                forward(way, part, what).start()
+
+    def index(part, keys):
+        def heads(j, sums):
+            raw = jnp.maximum(nn(keys, iq_all[j]), 0.0)
+            for i in range(8):
+                sums = sums + raw[:, i * 128 : i * 128 + 128] * iw_all[j, i : i + 1, :]
+            return sums
+
+        sums = lax.fori_loop(0, HEAD_DEVS, heads, jnp.zeros((PIECE, 128), F32))
+        wsum[part * 16 : part * 16 + 16] = (sums + pltpu.roll(sums, 64, 1)).reshape(16, PART, 128)
+
+    factor = (HEAD_DIM + ROPE) ** -0.5 * 1.4426950408889634
+
+    def attend(*pieces):
+        keys, scores, masks = [], [], []
+        for ahead_y, part in pieces:
+            origin = lax.rem(y + ahead_y, HEAD_DEVS)
+            keys.append(kv[origin, part * PIECE : part * PIECE + PIECE, :])
+            ropes = rp[origin, part * (PIECE // 2) : (part + 1) * (PIECE // 2), :]
+            scores += [nn(ropes, qra[...]), nn(ropes, qrb[...])]
+            masks.append(bias[part * PIECE : part * PIECE + PIECE, :])
+        keys = jnp.concatenate(keys, axis=0)
+        mask = jnp.concatenate(masks, axis=0)
+        scores = nn(keys, qlat[...]) + jnp.concatenate(scores, axis=0)
+        scores = scores + jnp.concatenate([mask] * (ROWS // 128), axis=1)
+        old = top[...]
+        new = jnp.maximum(old, jnp.max(scores, axis=0, keepdims=True))
+        expo = jnp.exp2((scores - new) * factor)
+        keep = jnp.exp2((old - new) * factor)
+        total[...] = total[...] * keep + jnp.sum(expo, axis=0, keepdims=True)
+        acc[...] = acc[...] * keep + nn(keys.T, expo.astype(BF))
+        top[...] = new
+
+    def arrived(first, last):
+        @pl.loop(first, last)
+        def _(s):
+            block_copy(s).wait_recv()
+
+    arrived(1, 40)
+    keys = compact(0)
     for d in range(1, HEAD_DEVS):
         iq_copy(d).wait_recv()
         iw_copy(d).wait_recv()
-
-    @pl.loop(0, 4)
-    def _(i):
-        keys_at = pl.ds(pl.multiple_of(i * 256, 256), 256)
-        keys = ukeys[keys_at, :]
-
-        def heads(j, sums):
-            part = lax.div(j, 4)
-            quad = lax.rem(j, 4)
-            queries = iq_all[part, pl.ds(pl.multiple_of(quad * 256, 256), 256), :]
-            raw = jnp.maximum(nt(keys, queries), 0.0)
-            return (
-                sums
-                + raw[:, :128] * iw_all[part, pl.ds(quad * 2, 1), :]
-                + raw[:, 128:] * iw_all[part, pl.ds(quad * 2 + 1, 1), :]
-            )
-
-        sums = lax.fori_loop(0, 16, heads, jnp.zeros((256, 128), F32))
-        wsum[pl.ds(pl.multiple_of(i * 16, 16), 16)] = (sums + pltpu.roll(sums, 64, 1)).reshape(
-            16, PART, 128
-        )
+    index(0, keys)
+    attend((0, 0))
+
+    arrived(40, 48)
+    keys = compact(1)
+    pass_on(0)
+    index(1, keys)
+    attend((0, 1), (3, 0), (1, 0))
+
+    arrived(48, 56)
+    keys = compact(2)
+    pass_on(1)
+    index(2, keys)
+    for way in range(2):
+        for what in range(2):
+            forward(way, 0, what).wait_recv()
+    attend((0, 2), (2, 0))
+    attend((3, 1), (1, 1))
+
+    arrived(56, 64)
+    keys = compact(3)
+    pass_on(2)
+    index(3, keys)
 
     @pl.loop(0, NSEL // 2)
     def _(i):
@@ -421,55 +466,28 @@
         picked_copy(d).start()
     picked_in[y] = picked[pl.ds(y * 4, 4)]
 
-    factor = (HEAD_DIM + ROPE) ** -0.5 * 1.4426950408889634
-
-    @pl.loop(0, 8)
-    def _(step):
-        for k, way, half in ((2, 0, 0), (3, 1, 0), (4, 0, 1), (5, 1, 1)):
-
-            @pl.when(step == k)
-            def _():
-                for what in range(2):
-                    direct(way, half, what).wait_recv()
-                    if way == half:
-                        forward(way, what).start()
-
-        for k, way in ((6, 0), (7, 1)):
-
-            @pl.when(step == k)
-            def _():
-                for what in range(2):
-                    forward(way, what).wait_recv()
-
-        side = jnp.where(lax.rem(step, 2) == 0, 3, 1)
-        ahead_y = jnp.where(step < 2, 0, jnp.where(step < 6, side, 2))
-        origin = lax.rem(y + ahead_y, HEAD_DEVS)
-        half = jnp.where(
-            step < 2, step, jnp.where(step < 6, lax.div(step - 2, 2), step - 6)
-        )
-
-        @pl.loop(0, 4)
-        def _(g):
-            at = pl.ds(pl.multiple_of(g * 256, 256), 256)
-            keys = kv[origin, half]
-            ropes = rp[origin, half]
-            scores = nt(qlat[at, :], keys)
-            scores = scores + jnp.concatenate([nt(qra[at, :], ropes), nt(qrb[at, :], ropes)], axis=1)
-            masked = bias[:, pl.ds(pl.multiple_of(half * HALF, HALF), HALF)]
-            scores = (scores.reshape(4, Q_DEV, HALF) + masked[None]).reshape(256, HALF)
-            old = top[at, :]
-            new = jnp.maximum(old, jnp.max(scores, axis=1, keepdims=True))
-            expo = jnp.exp2((scores - new) * factor)
-            keep = jnp.exp2((old - new) * factor)
-            total[at, :] = total[at, :] * keep + jnp.sum(expo, axis=1, keepdims=True)
-            acc[at, :] = acc[at, :] * keep + nn(expo.astype(BF), keys)
-            top[at, :] = new
-
-    cp_wuv.wait()
-    for h in range(HEADS_DEV):
-        at = slice(h * Q_DEV, h * Q_DEV + Q_DEV)
-        context = (acc[at, :] / total[at, :]).astype(BF)
-        attn_ref[:, h * HEAD_DIM : (h + 1) * HEAD_DIM] = nn(context, wuv_v[h]).astype(BF)
+    for way in range(2):
+        for what in range(2):
+            forward(way, 1, what).wait_recv()
+    attend((0, 3), (2, 1))
+    attend((3, 2), (1, 2))
+    pass_on(3)
+    for way in range(2):
+        for what in range(2):
+            forward(way, 2, what).wait_recv()
+    attend((2, 2), (3, 3), (1, 3))
+    for way in range(2):
+        for what in range(2):
+            forward(way, 3, what).wait_recv()
+    attend((2, 3))
+
+    for m in range(HEADS_DEV // 2):
+        at = slice(m * 128, m * 128 + 128)
+        context = (acc[:, at] / total[:, at]).astype(BF)
+        both = nn(wuv_t[2 * m : 2 * m + 2].reshape(256, LATENT), context)
+        joined = jnp.where(low, both[:128], both[128:]).T
+        attn_ref[:, 2 * m * HEAD_DIM : (2 * m + 1) * HEAD_DIM] = joined[:Q_DEV].astype(BF)
+        attn_ref[:, (2 * m + 1) * HEAD_DIM : (2 * m + 2) * HEAD_DIM] = joined[Q_DEV:].astype(BF)
 
     for d in range(1, HEAD_DEVS):
         picked_copy(d).wait_recv()
@@ -489,9 +507,9 @@
         picked_copy(d).wait_send()
     for way in range(2):
         for what in range(2):
-            for half in range(2):
-                direct(way, half, what).wait_send()
-            forward(way, what).wait_send()
+            for part in range(PARTS):
+                direct(way, part, what).wait_send()
+                forward(way, part, what).wait_send()
 
 
 def shards(
@@ -510,11 +528,12 @@
         in_specs=[vmem] * 4 + [hbm] * 5,
         out_specs=(vmem, vmem),
         scratch_shapes=[
-            pltpu.VMEM((BLK_DEV, PART, width), BF),
+            pltpu.VMEM((width, BLK_DEV * BLOCK), BF),
             pltpu.VMEM(query.shape, BF),
             pltpu.VMEM(index_query.shape, BF),
             pltpu.VMEM(w_uk.shape, BF),
             pltpu.VMEM(w_uv.shape, BF),
+            pltpu.VMEM((HEADS_DEV, HEAD_DIM, LATENT), BF),
             pltpu.VMEM((CTX_DEVS, 1, 128), F32),
             pltpu.VMEM((CTX_DEVS, 1, 128), F32),
             pltpu.VMEM((BLK_DEV * PART, LATENT + 384), BF),
@@ -522,23 +541,22 @@
             pltpu.VMEM((CTX_DEVS, PART, PAIR), BF),
             pltpu.VMEM((CTX_DEVS, PART, PAIR), BF),
             pltpu.VMEM((NSEL // 2, 128), F32),
-            pltpu.VMEM((Q_DEV, PART_KEYS), F32),
+            pltpu.VMEM((PART_KEYS, 128), F32),
             pltpu.VMEM((POOL, PART_KEYS), F32),
             pltpu.VMEM((POOL, PART_KEYS), F32),
-            pltpu.VMEM((PART_KEYS, IDX_DIM), BF),
-            pltpu.VMEM((HEAD_DEVS, 2, HALF, LATENT), BF),
-            pltpu.VMEM((HEAD_DEVS, 2, HALF // 2, 128), BF),
-            pltpu.VMEM((HEAD_DEVS, ROWS, IDX_DIM), BF),
+            pltpu.VMEM((HEAD_DEVS, PART_KEYS, LATENT), BF),
+            pltpu.VMEM((HEAD_DEVS, PART_KEYS // 2, 128), BF),
+            pltpu.VMEM((HEAD_DEVS, IDX_DIM, ROWS), BF),
             pltpu.VMEM((HEAD_DEVS, 8, 128), F32),
-            pltpu.VMEM((ROWS, LATENT), BF),
-            pltpu.VMEM((ROWS, 128), BF),
-            pltpu.VMEM((ROWS, 128), BF),
+            pltpu.VMEM((LATENT, ROWS), BF),
+            pltpu.VMEM((128, ROWS), BF),
+            pltpu.VMEM((128, ROWS), BF),
             pltpu.VMEM((POOL, PART, 128), F32),
             pltpu.VMEM((NSEL // 2, PART, 128), F32),
             pltpu.VMEM((HEAD_DEVS, NSEL // 8, PART, 128), F32),
-            pltpu.VMEM((ROWS, 1), F32),
-            pltpu.VMEM((ROWS, 1), F32),
-            pltpu.VMEM((ROWS, LATENT), F32),
+            pltpu.VMEM((1, ROWS), F32),
+            pltpu.VMEM((1, ROWS), F32),
+            pltpu.VMEM((LATENT, ROWS), F32),
             dma((5,)),
             dma((CTX_DEVS,)),
             dma((CTX_DEVS,)),
@@ -550,22 +568,22 @@
             dma((3,)),
             dma((3,)),
             dma((3,)),
-            dma((2, 2, 2)),
-            dma((2, 2, 2)),
-            dma((2, 2)),
-            dma((2, 2)),
+            dma((2, PARTS, 2)),
+            dma((2, PARTS, 2)),
+            dma((2, PARTS, 2)),
+            dma((2, PARTS, 2)),
         ],
         compiler_params=pltpu.CompilerParams(
             collective_id=0, has_side_effects=True, vmem_limit_bytes=58 * 1024 * 1024
         ),
     )(
-        selected.T.reshape(1, Q_DEV * NSEL),
+        selected.T,
         block_home.reshape(1, NBLK),
-        key_scale.reshape(BLK_DEV, BLOCK),
-        index_weight.T.reshape(8, 128),
+        key_scale.reshape(1, BLK_DEV * BLOCK),
+        index_weight.T,
         query,
         index_query,
-        cache_rows.reshape(BLK_DEV, BLOCK, width),
+        cache_rows.T,
         w_uk,
         w_uv,
     )

time: 157 us -> 123 us (0.78)
  Pallas kernels: 144 us -> 118 us
  local copies, waits for them, and re-layouts: 12 us -> 3.26 us
    pallas_call x1, Pallas kernels: 144 us -> 118 us  [shards(): pl.pallas_call(kernel, out_shape=(jax.ShapeDtypeStruct((Q_DEV, HEADS_DEV...]
    unnamed x3 -> x2, local copies, waits for them, and re-layouts: 7.86 us -> 3.26 us
    reshape x3 -> x0, local copies, waits for them, and re-layouts: 4.12 us -> none  [the longest x1 1.39 us: shards(): selected.T.reshape(1, Q_DEV * NSEL)]
where the time goes in v2:
time: 123 us; the launch traced here: 122 us
  Pallas kernels  118 us (96%)
  local copies, waits for them, and re-layouts  3.26 us (3%)
    pallas_call x1, Pallas kernels, shards(): pl.pallas_call(kernel, out_shape=(jax.ShapeDtypeStruct((Q_DEV, HEADS_DEV...  118 us
    unnamed x2, local copies, waits for them, and re-layouts  3.26 us

profile of v2, /device:TPU:1, one launch (start us, length us, event | category | flops | bytes accessed | tf_op | source)
XLA Modules:
  0.0 121.9 jit_solution(17910537904709758957)
XLA Ops:
  0.6 118.0 %shard_map.104 = (bf16[64,2048]{1,0:T(8,128)(2,1)}, f32[64,512]{1,0:T(8,128)}) custom-call(s32[32,64]{1,0:T(8,128)} %bitcast.10, s32[1,2048]{1,0:T(1,128)} %bitcast.11, f32[1,2048]{1,0:T(1,128)} %bitcast.12, f32[16,64]{1,0:T(8,128)} %bitcast.13, bf16[64,16,192]{2,1,0:T(8,128)(2,1)} %query_hbm.1, bf16[64,16,128]{2,1,0:T(8,128)(2,1)} %iq_hbm.1, ...), custom_call_target="tpu_custom_call" | custom-call | tf_op jit(solution)/shard_map/pallas_call | solution.py:522
  118.6 1.7 %copy.11 = bf16[8,8,16,128]{3,2,1,0:T(8,128)(2,1)} copy(bf16[8,8,16,128]{3,1,2,0:T(8,128)(2,1)} %bitcast.9) | data formatting | bytes 524288
  120.3 1.6 %copy.13 = f32[64,512]{1,0:T(8,128)} copy(f32[64,512]{1,0:T(8,128)} %get-tuple-element.9) | data formatting | bytes 262144

commit v3 on v2

--- a/solution.py
+++ b/solution.py
@@ -106,8 +106,17 @@
     me = lax.axis_index("ctx")
     y = lax.axis_index("head")
 
-    def ctx_peer(c):
-        return (lax.rem(c + 2 * CTX_DEVS, CTX_DEVS), y)
+    my_x, my_z, my_core = lax.div(me, 16), lax.rem(lax.div(me, 2), 8), lax.rem(me, 2)
+
+    def ctx_peer(s, way):
+        turn = lax.div(s, 8)
+        odd = lax.rem(turn, 2)
+        dz = odd * lax.div(turn + 1, 2) + (1 - odd) * lax.rem(8 - lax.div(turn, 2), 8)
+        dx = lax.rem(lax.div(s, 2), 4)
+        to_x = lax.rem(my_x + way * dx + 4, 4)
+        to_z = lax.rem(my_z + way * dz + 8, 8)
+        to_core = lax.rem(my_core + s, 2)
+        return ((to_x * 8 + to_z) * 2 + to_core, y)
 
     def head_peer(d):
         return (me, lax.rem(y + d, HEAD_DEVS))
@@ -116,7 +125,7 @@
 
     @pl.loop(1, CTX_DEVS)
     def _(s):
-        pl.semaphore_signal(barrier, inc=1, device_id=ctx_peer(me + s), device_id_type=MESH)
+        pl.semaphore_signal(barrier, inc=1, device_id=ctx_peer(s, 1), device_id_type=MESH)
 
     for d in range(1, HEAD_DEVS):
         pl.semaphore_signal(barrier, inc=1, device_id=head_peer(d), device_id_type=MESH)
@@ -126,8 +135,7 @@
     cp_iq = pltpu.make_async_copy(iq_hbm, iq_v, local_sem.at[2])
     cp_wuk = pltpu.make_async_copy(wuk_hbm, wuk_v, local_sem.at[3])
     cp_wuv = pltpu.make_async_copy(wuv_hbm, wuv_v, local_sem.at[4])
-    for cp in (cp_cache, cp_query, cp_iq, cp_wuk, cp_wuv):
-        cp.start()
+    cp_cache.start()
 
     sel = jnp.concatenate([sel_ref[i : i + 1, :] for i in range(NSEL)], axis=1)
     home = home_ref[...]
@@ -139,7 +147,10 @@
     counts = nt(sel_hi, sel_lo)
     wanted = onehot(counts > 0.5)
     wanted_row = jnp.sum(nn(wanted, log_lo) * log_hi.astype(F32), axis=0, keepdims=True)
-    rel = (me - (home >> 5)) & (CTX_DEVS - 1)
+    owner = home >> 5
+    dz = (my_z - ((owner >> 1) & 7)) & 7
+    turn = jnp.where(dz == 0, 0, jnp.where(dz <= 4, 2 * dz - 1, 16 - 2 * dz))
+    rel = turn * 8 + ((my_x - (owner >> 4)) & 3) * 2 + ((my_core - owner) & 1)
     holder = jnp.where(iota((CTX_DEVS, NBLK), 0) == rel, 1.0, 0.0)
     slot = onehot(iota((128, NBLK), 0) == (home & (BLK_DEV - 1)))
     want_rel = nt((holder * wanted_row).astype(BF), slot)
@@ -154,7 +165,7 @@
             dst_ref=want_in.at[s],
             send_sem=req_send.at[s],
             recv_sem=req_recv.at[s],
-            device_id=ctx_peer(me - s),
+            device_id=ctx_peer(s, -1),
             device_id_type=MESH,
         )
 
@@ -163,6 +174,8 @@
         request(s).start()
 
     cp_cache.wait()
+    for cp in (cp_query, cp_iq, cp_wuk, cp_wuv):
+        cp.start()
     row = iota((BLK_DEV * PART, NBLK), 0)
     mine = onehot(iota((BLK_DEV * PART, NBLK), 1) == (row >> 4) * BLOCK + y * PART + (row & 15))
     scaled = (cache_v[LATENT + ROPE :, :].astype(F32) * scale_ref[...]).astype(BF)
@@ -192,7 +205,7 @@
             dst_ref=recv.at[s],
             send_sem=blk_send.at[s],
             recv_sem=blk_recv.at[s],
-            device_id=ctx_peer(me + s),
+            device_id=ctx_peer(s, 1),
             device_id_type=MESH,
         )
 

time: 123 us -> 135 us (1.098)
  the two profiles are of different devices: /device:TPU:1 before, /device:TPU:6 now
where the time goes in v3:
time: 135 us
  Pallas kernels  131 us (97%)
  local copies, waits for them, and re-layouts  3.26 us (2%)
    pallas_call x1, Pallas kernels, shards(): pl.pallas_call(kernel, out_shape=(jax.ShapeDtypeStruct((Q_DEV, HEADS_DEV...  131 us
    unnamed x2, local copies, waits for them, and re-layouts  3.26 us

profile of v3, /device:TPU:6, one launch (start us, length us, event | category | flops | bytes accessed | tf_op | source)
XLA Modules:
  0.0 134.7 jit_solution(3003323342593394242)
XLA Ops:
  0.6 130.8 %shard_map.104 = (bf16[64,2048]{1,0:T(8,128)(2,1)}, f32[64,512]{1,0:T(8,128)}) custom-call(s32[32,64]{1,0:T(8,128)} %bitcast.10, s32[1,2048]{1,0:T(1,128)} %bitcast.11, f32[1,2048]{1,0:T(1,128)} %bitcast.12, f32[16,64]{1,0:T(8,128)} %bitcast.13, bf16[64,16,192]{2,1,0:T(8,128)(2,1)} %query_hbm.1, bf16[64,16,128]{2,1,0:T(8,128)(2,1)} %iq_hbm.1, ...), custom_call_target="tpu_custom_call" | custom-call | tf_op jit(solution)/shard_map/pallas_call | solution.py:535
  131.4 1.7 %copy.11 = bf16[8,8,16,128]{3,2,1,0:T(8,128)(2,1)} copy(bf16[8,8,16,128]{3,1,2,0:T(8,128)(2,1)} %bitcast.9) | data formatting | bytes 524288
  133.1 1.6 %copy.13 = f32[64,512]{1,0:T(8,128)} copy(f32[64,512]{1,0:T(8,128)} %get-tuple-element.9) | data formatting | bytes 262144

commit v4 on v2

--- a/solution.py
+++ b/solution.py
@@ -126,8 +126,7 @@
     cp_iq = pltpu.make_async_copy(iq_hbm, iq_v, local_sem.at[2])
     cp_wuk = pltpu.make_async_copy(wuk_hbm, wuk_v, local_sem.at[3])
     cp_wuv = pltpu.make_async_copy(wuv_hbm, wuv_v, local_sem.at[4])
-    for cp in (cp_cache, cp_query, cp_iq, cp_wuk, cp_wuv):
-        cp.start()
+    cp_cache.start()
 
     sel = jnp.concatenate([sel_ref[i : i + 1, :] for i in range(NSEL)], axis=1)
     home = home_ref[...]
@@ -163,6 +162,8 @@
         request(s).start()
 
     cp_cache.wait()
+    for cp in (cp_query, cp_iq, cp_wuk, cp_wuv):
+        cp.start()
     row = iota((BLK_DEV * PART, NBLK), 0)
     mine = onehot(iota((BLK_DEV * PART, NBLK), 1) == (row >> 4) * BLOCK + y * PART + (row & 15))
     scaled = (cache_v[LATENT + ROPE :, :].astype(F32) * scale_ref[...]).astype(BF)
@@ -476,6 +477,13 @@
         for what in range(2):
             forward(way, 2, what).wait_recv()
     attend((2, 2), (3, 3), (1, 3))
+    for d in range(1, HEAD_DEVS):
+        picked_copy(d).wait_recv()
+    for i in range(4):
+        even = jnp.concatenate([picked_in[j, i] for j in range(HEAD_DEVS)], axis=0)
+        both = jnp.concatenate([even, pltpu.roll(even, 64, 1)], axis=0)
+        idx_ref[:, i * 128 : (i + 1) * 128] = both.T[:Q_DEV, :]
+
     for way in range(2):
         for what in range(2):
             forward(way, 3, what).wait_recv()
@@ -488,13 +496,6 @@
         joined = jnp.where(low, both[:128], both[128:]).T
         attn_ref[:, 2 * m * HEAD_DIM : (2 * m + 1) * HEAD_DIM] = joined[:Q_DEV].astype(BF)
         attn_ref[:, (2 * m + 1) * HEAD_DIM : (2 * m + 2) * HEAD_DIM] = joined[Q_DEV:].astype(BF)
-
-    for d in range(1, HEAD_DEVS):
-        picked_copy(d).wait_recv()
-    for i in range(4):
-        even = jnp.concatenate([picked_in[j, i] for j in range(HEAD_DEVS)], axis=0)
-        both = jnp.concatenate([even, pltpu.roll(even, 64, 1)], axis=0)
-        idx_ref[:, i * 128 : (i + 1) * 128] = both.T[:Q_DEV, :]
 
     @pl.loop(1, CTX_DEVS)
     def _(s):

time: 123 us -> 123 us (level)
  no operation moved by 1% of the time
where the time goes in v4:
time: 123 us; the launch traced here: 122 us
  Pallas kernels  118 us (96%)
  local copies, waits for them, and re-layouts  3.26 us (3%)
    pallas_call x1, Pallas kernels, shards(): pl.pallas_call(kernel, out_shape=(jax.ShapeDtypeStruct((Q_DEV, HEADS_DEV...  118 us
    unnamed x2, local copies, waits for them, and re-layouts  3.26 us

profile of v4, /device:TPU:1, one launch (start us, length us, event | category | flops | bytes accessed | tf_op | source)
XLA Modules:
  0.0 121.9 jit_solution(13774620161204122333)
XLA Ops:
  0.6 118.0 %shard_map.104 = (bf16[64,2048]{1,0:T(8,128)(2,1)}, f32[64,512]{1,0:T(8,128)}) custom-call(s32[32,64]{1,0:T(8,128)} %bitcast.10, s32[1,2048]{1,0:T(1,128)} %bitcast.11, f32[1,2048]{1,0:T(1,128)} %bitcast.12, f32[16,64]{1,0:T(8,128)} %bitcast.13, bf16[64,16,192]{2,1,0:T(8,128)(2,1)} %query_hbm.1, bf16[64,16,128]{2,1,0:T(8,128)(2,1)} %iq_hbm.1, ...), custom_call_target="tpu_custom_call" | custom-call | tf_op jit(solution)/shard_map/pallas_call | solution.py:523
  118.7 1.7 %copy.11 = bf16[8,8,16,128]{3,2,1,0:T(8,128)(2,1)} copy(bf16[8,8,16,128]{3,1,2,0:T(8,128)(2,1)} %bitcast.9) | data formatting | bytes 524288
  120.3 1.6 %copy.13 = f32[64,512]{1,0:T(8,128)} copy(f32[64,512]{1,0:T(8,128)} %get-tuple-element.9) | data formatting | bytes 262144
